TPU v7x, 32 devices: a whole 2x2x4 slice. The times are simulated.
32 devices in a mesh: section: 2 (over core), dp: 8 (over z, x), mp: 2 (over y).
Axes of the slice: x: 2, y: 2, z: 4, core: 2. Of those that a mesh axis runs over, the one named last changes fastest.
Arguments:
- section_weights: bfloat16 [2, 12288, 12288], P('section', 'mp', 'dp'), may hold values from -0.0546875 to 0.0546875
- tensor_inputs: bfloat16 [2, 1024, 12288], P('section', 'dp', 'mp'), may hold values from -6 to 6
- stream_inputs: bfloat16 [2, 1024, 12288], P('section', 'mp', 'dp'), may hold values from -26 to 26
- ln_gain: float32 [12288], P('dp'), may hold values from 0.5 to 1.5
- ln_bias: float32 [12288], P('dp'), may hold values from -3 to 3
Outputs:
- handed_over: bfloat16 [2, 1024, 12288], P('section', 'mp', 'dp')
- section_outputs: bfloat16 [2, 1024, 12288], P('section', 'dp', 'mp')
All inputs are finite; a program needn't handle non-finite values.
Results may differ from a plain program's by a relative error of at most 0.0056.
Values may be sent and summed in bfloat16 or wider, within the bound.
A program may use at most 128 MiB of HBM per device.

v0:
```python
import jax
import jax.numpy as jnp
from jax import lax
from jax.sharding import PartitionSpec as P

D = 12288


def passed_along(x, axis, by):
    size = lax.axis_size(axis)
    return lax.ppermute(x, axis, [(i, (i + by) % size) for i in range(size)])


def moments(values):
    first_sum, square_sum = lax.psum(
        (jnp.sum(values, axis=1), jnp.sum(values * values, axis=1)), "dp"
    )
    center = first_sum[:, None] / D
    spread = square_sum[:, None] / D - center * center
    return (center, lax.rsqrt(spread + 1e-05))


def normalize(values, ln_gain, ln_bias):
    widened = values.astype(jnp.float32)
    center, inverse = moments(widened)
    return ((widened - center) * inverse * ln_gain + ln_bias).astype(jnp.bfloat16)


def contract(left, weight):
    return lax.dot_general(
        left, weight, (((1,), (1,)), ((), ())), preferred_element_type=jnp.float32
    )


def summed_output(product):
    return lax.psum_scatter(product, "dp", scatter_dimension=0, tiled=True)


def local(section_weights, tensor_inputs, stream_inputs, ln_gain, ln_bias):
    second_section = lax.axis_index("section") == 1
    weight = section_weights[0]
    incoming = tensor_inputs[0]
    saved = stream_inputs[0].astype(jnp.float32)
    partial_sums = jnp.dot(
        lax.all_gather(incoming, "dp", axis=0, tiled=True),
        weight,
        preferred_element_type=jnp.float32,
    )
    summed = lax.psum_scatter(partial_sums, "mp", scatter_dimension=0, tiled=True)
    center, inverse = moments(saved)
    normed = (saved - center) * inverse
    scaled = summed * ln_gain
    first_total, second_total = lax.psum(
        (jnp.sum(scaled, axis=1), jnp.sum(scaled * normed, axis=1)), "dp"
    )
    grad_in = inverse * (scaled - first_total[:, None] / D - normed * (second_total[:, None] / D))
    outgoing = jnp.where(second_section, grad_in, summed + saved).astype(jnp.bfloat16)
    own_rows = passed_along(outgoing, "section", 1)
    operand = jnp.where(second_section, normalize(own_rows, ln_gain, ln_bias), own_rows)
    product = contract(lax.all_gather(operand, "mp", axis=0, tiled=True), weight)
    result = summed_output(product)
    return (own_rows[None], result.astype(jnp.bfloat16)[None])


def solution(mesh):
    in_specs = (
        P("section", "mp", "dp"),
        P("section", "dp", "mp"),
        P("section", "mp", "dp"),
        P("dp"),
        P("dp"),
    )
    out_specs = (P("section", "mp", "dp"), P("section", "dp", "mp"))
    return jax.shard_map(local, mesh=mesh, in_specs=in_specs, out_specs=out_specs, check_vma=False)
```

profile of v0, /device:TPU:21, one launch (start us, length us, event | category | flops | bytes accessed | tf_op | source)
XLA Modules:
  0.0 823.4 jit_solution(1729005518829507261)
XLA Ops:
  7.2 0.0 all-gather.6.cloned.1.call-start
  7.2 0.7 all-gather.6.cloned.1.call-update
  7.9 0.0 reduce-scatter.3.cloned.1.call-start
  7.9 178.4 %all-gather.6.cloned.1.call-done = bf16[1,1024,6144]{2,1,0:T(8,128)(2,1)} async-done(((bf16[1,128,6144]{2,1,0:T(8,128)(2,1)}), bf16[1,1024,6144]{2,1,0:T(8,128)(2,1)}) %all-gather.6.cloned.1.call-update) | async-done | bytes 12582928 | tf_op jit(solution)/shard_map/all_gather | solution.py:45
  186.4 26.2 %fusion.2 = f32[1024,1536]{1,0:T(8,128)} fusion(bf16[1,6144,1536]{2,1,0:T(8,128)(2,1)} %param.5, bf16[1,1024,6144]{2,1,0:T(8,128)(2,1)} %all-gather.6.cloned.1.call-done), kind=kOutput, calls=%fused_computation.2 | convolution fusion | flops 19327352832 | bytes 37748736 | tf_op jit(solution)/shard_map/dot_general | solution.py:44
  212.5 0.0 copy-start
  212.6 0.0 reduce-scatter.3.cloned.1.call-update
  212.6 0.0 copy-start.1
  212.6 0.0 all-gather.4.cloned.1.call-start
  212.6 1.3 copy-done
  214.0 0.3 convert_reduce_fusion.1
  214.2 0.4 fusion.8
  214.6 11.6 %all-reduce.2 = (f32[512]{0:T(512)S(1)}, f32[512]{0:T(512)S(1)}) all-reduce(f32[512]{0:T(512)S(1)} %fusion.8, f32[512]{0:T(512)S(1)} %convert_reduce_fusion.1), channel_id=1, replica_groups=mesh['section'=2,'dp'=8,'mp'=2] {'dp'}, use_global_device_ids=true, to_apply=%region_1.0 | all-reduce | flops 1024 | bytes 8192 | tf_op jit(solution)/shard_map/psum | solution.py:15
  226.3 62.1 %reduce-scatter.3.cloned.1.call-done = f32[512,1536]{1,0:T(8,128)} async-done(((f32[1024,1536]{1,0:T(8,128)}), f32[512,1536]{1,0:T(8,128)}) %reduce-scatter.3.cloned.1.call-update) | async-done | bytes 3145744 | tf_op jit(solution)/shard_map/reduce_scatter | solution.py:49
  288.4 0.0 copy-done.1
  288.4 2.9 multiply_reduce_fusion
  291.2 12.3 %all-reduce.1 = (f32[512]{0:T(512)S(1)}, f32[512]{0:T(512)S(1)}) all-reduce(f32[512]{0:T(512)S(1)} %get-tuple-element.3, f32[512]{0:T(512)S(1)} %get-tuple-element.2), channel_id=1, replica_groups=mesh['section'=2,'dp'=8,'mp'=2] {'dp'}, use_global_device_ids=true, to_apply=%region_8.0 | all-reduce | flops 1024 | bytes 8192 | tf_op jit(solution)/shard_map/psum | solution.py:53
  303.5 0.0 copy-start.2
  303.5 2.8 fusion.16
  306.3 4.4 collective-permute-start
  310.7 3.0 collective-permute-done
  313.7 0.6 convert_reduce_fusion
  314.3 14.6 %all-reduce = (f32[512]{0:T(512)S(1)}, f32[512]{0:T(512)S(1)}) all-reduce(f32[512]{0:T(512)S(1)} %get-tuple-element.5, f32[512]{0:T(512)S(1)} %get-tuple-element.4), channel_id=1, replica_groups=mesh['section'=2,'dp'=8,'mp'=2] {'dp'}, use_global_device_ids=true, to_apply=%region_12.13 | all-reduce | flops 1024 | bytes 8192 | tf_op jit(solution)/shard_map/psum | solution.py:15
  328.9 0.0 copy-done.2
  328.9 2.0 fusion.22
  330.9 0.0 all-gather.4.cloned.1.call-update
  330.9 0.0 reduce-scatter.5.cloned.1.call-start
  331.0 50.5 %all-gather.4.cloned.1.call-done = bf16[1024,1536]{1,0:T(8,128)(2,1)} async-done(((bf16[512,1536]{1,0:T(8,128)(2,1)}), bf16[1024,1536]{1,0:T(8,128)(2,1)}) %all-gather.4.cloned.1.call-update) | async-done | bytes 3145744 | tf_op jit(solution)/shard_map/all_gather | solution.py:60
  381.5 26.3 %fusion = f32[1024,6144]{1,0:T(8,128)} fusion(bf16[1024,1536]{1,0:T(8,128)(2,1)} %all-gather.4.cloned.1.call-done, bf16[1,6144,1536]{2,1,0:T(8,128)(2,1)} %param.5), kind=kOutput, calls=%fused_computation | convolution fusion | flops 19327352832 | bytes 47185920 | tf_op jit(solution)/shard_map/dot_general | solution.py:30
  407.8 0.0 reduce-scatter.5.cloned.1.call-update
  407.8 404.7 %reduce-scatter.5.cloned.1.call-done = f32[128,6144]{1,0:T(8,128)} async-done(((f32[1024,6144]{1,0:T(8,128)}), f32[128,6144]{1,0:T(8,128)}) %reduce-scatter.5.cloned.1.call-update) | async-done | bytes 3145744 | tf_op jit(solution)/shard_map/reduce_scatter | solution.py:36
  812.6 3.2 convert_bitcast_fusion.1
  815.8 1.1 copy.8
  (3 shorter events, 0.0 us)
Async XLA Ops:
  7.2 179.2 %all-gather.6.cloned.1.call-start = ((), (), s32[]{:S(2)}) async-start(), calls=%async_computation.5 | async-start | bytes 14155776 | tf_op jit(solution)/shard_map/all_gather | solution.py:45
  7.9 280.5 %reduce-scatter.3.cloned.1.call-start = ((), (), s32[]{:S(2)}) async-start(), calls=%async_computation.2 | async-start | bytes 9437184 | tf_op jit(solution)/shard_map/reduce_scatter | solution.py:49
  212.5 1.4 copy-start
  212.6 75.8 %copy-start.1 = (f32[1536]{0:T(1024)S(1)}, f32[1536]{0:T(1024)}, u32[]{:S(2)}) copy-start(f32[1536]{0:T(1024)} %param.8) | copy-start | bytes 18436
  212.6 168.9 %all-gather.4.cloned.1.call-start = ((), (), s32[]{:S(2)}) async-start(), calls=%async_computation.3 | async-start | bytes 4718592 | tf_op jit(solution)/shard_map/all_gather | solution.py:60
  303.5 25.4 %copy-start.2 = (f32[1536]{0:T(1024)S(1)}, f32[1536]{0:T(1024)}, u32[]{:S(2)}) copy-start(f32[1536]{0:T(1024)} %param.9) | copy-start | bytes 18436
  306.3 7.4 collective-permute-start
  330.9 481.6 %reduce-scatter.5.cloned.1.call-start = ((), (), s32[]{:S(2)}) async-start(), calls=%async_computation.4 | async-start | bytes 28311552 | tf_op jit(solution)/shard_map/reduce_scatter | solution.py:36
Sparse Core Ops, SparseCore 0:
  10.2 176.1 all-gather.5
  212.7 75.6 reduce-scatter.2
  331.1 50.3 all-gather.3
  408.0 404.5 reduce-scatter.4
where the time goes:
time: 826 us; the launch traced here: 823 us
  waiting for transfers between devices  699 us (85%)
  matrix products  52.5 us (6%)
  blocking collectives  38.5 us (5%)
  between operations  13.8 us (2%)
  other arithmetic  12.1 us (1%)
    reduce_scatter x1, waiting for transfers between devices, summed_output(): return lax.psum_scatter(product, 'dp', scatter_dimension=0, tiled=True)  405 us
    all_gather x1, waiting for transfers between devices, local(): lax.all_gather(incoming, 'dp', axis=0, tiled=True)  178 us
    reduce_scatter x1, waiting for transfers between devices, local(): lax.psum_scatter(partial_sums, 'mp', scatter_dimension=0, tiled=True)  62.1 us
    all_gather x1, waiting for transfers between devices, local(): lax.all_gather(operand, 'mp', axis=0, tiled=True)  50.5 us
    dot_general x1, matrix products, contract(): lax.dot_general(left, weight, (((1,), (1,)), ((), ())), preferred_element...  26.3 us
    psum x2, blocking collectives, moments(): lax.psum((jnp.sum(values, axis=1), jnp.sum(values * values, axis=1)), 'dp')  26.2 us
    dot_general x1, matrix products, local(): jnp.dot(lax.all_gather(incoming, 'dp', axis=0, tiled=True), weight, prefe...  26.2 us
  transfers between devices with their start and end apart: 5, of which 5 were waited for; matrix products, arithmetic and copies ran while one was open for 0% of the time, Pallas kernels for 0%

commit v1 on v0

--- a/solution.py
+++ b/solution.py
@@ -1,9 +1,14 @@
+import functools
+
 import jax
 import jax.numpy as jnp
 from jax import lax
+from jax.experimental import pallas as pl
+from jax.experimental.pallas import tpu as pltpu
 from jax.sharding import PartitionSpec as P
 
 D = 12288
+MESH = pl.DeviceIdType.MESH
 
 
 def passed_along(x, axis, by):
@@ -62,7 +67,445 @@
     return (own_rows[None], result.astype(jnp.bfloat16)[None])
 
 
+ARRIVALS = (
+    (0, 1, 4, 2, 5, 3, 6, 7),
+    (1, 2, 0, 5, 3, 6, 4, 7),
+    (2, 1, 3, 6, 0, 5, 7, 4),
+    (3, 2, 7, 1, 6, 0, 5, 4),
+)
+DESTINATIONS = ((3, 2, 1, 0), (3, 2, 0, 1), (0, 1, 3, 2), (0, 1, 2, 3))
+
+
+def by_place(z, table):
+    codes = [sum(entry * 8**i for i, entry in enumerate(row)) for row in table]
+    code = jnp.int32(codes[0])
+    for place in range(1, 4):
+        code = jnp.where(z == place, jnp.int32(codes[place]), code)
+    return code
+
+
+def as_rows(first, second):
+    lane = lax.broadcasted_iota(jnp.int32, (128, 128), 1)
+    return jnp.where(lane == 0, first, second).T[0:8]
+
+
+def as_columns(rows):
+    square = jnp.concatenate([rows] * 16, axis=0).T
+    return square[:, 0:1], square[:, 1:2]
+
+
+def kernel(
+    w_hbm, x_hbm, saved, gain, bias, handed, result,
+    w, gath, kept, y_out, y_in, rows, operand, operands, x_in, z_in,
+    stat_a, stat_b,
+    local_sem, ag_recv, ag_x, ag_up, ag_down, y_send, y_recv,
+    a_send, a_recv, b_send, b_recv,
+    h_send, h_recv, o_send, o_cross, o_recv, xs_send, xs_recv, zs_send, zs_recv,
+):
+    s, d, m = lax.axis_index("section"), lax.axis_index("dp"), lax.axis_index("mp")
+    z, x = d // 2, d % 2
+    first_section = s == 0
+    width = w.shape[1]
+    depth = w.shape[0]
+    f32, bf16 = jnp.float32, jnp.bfloat16
+
+    def block(j, n=1):
+        return pl.ds(pl.multiple_of(j * 128, 128), 128 * n)
+
+    def columns(n, size):
+        return pl.ds(pl.multiple_of(n * size, size), size)
+
+    def remote(src, dst, send, recv, **where):
+        return pltpu.make_async_remote_copy(
+            src_ref=src, dst_ref=dst, send_sem=send, recv_sem=recv,
+            device_id=where, device_id_type=MESH,
+        )
+
+    load_w = pltpu.make_async_copy(w_hbm, w, local_sem.at[0])
+    load_x = pltpu.make_async_copy(x_hbm, gath.at[block(d)], local_sem.at[1])
+    load_w.start()
+    load_x.start()
+
+    barrier = pltpu.get_barrier_semaphore()
+    for k in range(1, 8):
+        pl.semaphore_signal(barrier, inc=1, device_id={"dp": (d + k) % 8}, device_id_type=MESH)
+    pl.semaphore_signal(barrier, inc=1, device_id={"mp": 1 - m}, device_id_type=MESH)
+    pl.semaphore_signal(barrier, inc=1, device_id={"section": 1 - s}, device_id_type=MESH)
+    pl.semaphore_signal(
+        barrier, inc=1, device_id={"section": 1 - s, "mp": 1 - m}, device_id_type=MESH
+    )
+    pl.semaphore_wait(barrier, 10)
+    load_x.wait()
+
+    def over_x(j, zj):
+        return remote(gath.at[block(j)], gath.at[block(j)], ag_x.at[zj], ag_recv.at[j], dp=d + 1 - 2 * x)
+
+    def upward(j, zj):
+        return remote(gath.at[block(j)], gath.at[block(j)], ag_up.at[zj], ag_recv.at[j], dp=(d + 2) % 8)
+
+    def downward(j, zj):
+        return remote(gath.at[block(j)], gath.at[block(j)], ag_down.at[zj], ag_recv.at[j], dp=(d + 6) % 8)
+
+    def y_copy(r):
+        return remote(y_out.at[block(r)], y_in.at[block(r)], y_send.at[r], y_recv.at[r], mp=1 - m)
+
+    def send_stats(stats, send, recv, start):
+        for k in range(1, 8):
+            c = remote(stats.at[d], stats.at[d], send.at[k], recv.at[d], dp=(d + k) % 8)
+            if start:
+                c.start()
+            else:
+                c.wait_send()
+
+    def receive_stats(stats, send, recv):
+        for k in range(1, 8):
+            e = (d + k) % 8
+            remote(stats.at[e], stats.at[e], send.at[k], recv.at[e], dp=e).wait_recv()
+
+    def forward(j, zj):
+        @pl.when((zj <= z) & (z < 3))
+        def _():
+            upward(j, zj).start()
+
+        @pl.when((zj >= z) & (z > 0))
+        def _():
+            downward(j, zj).start()
+
+        over_x(j, zj).start()
+
+    forward(d, z)
+
+    def saved_sums(r, carry):
+        v = saved[block(r), :].astype(f32)
+        tile = as_rows(
+            jnp.sum(v, axis=1, keepdims=True), jnp.sum(v * v, axis=1, keepdims=True)
+        )
+        stat_a[d, pl.ds(pl.multiple_of(r * 8, 8), 8), :] = tile
+        return carry
+
+    lax.fori_loop(0, 4, saved_sums, 0)
+    send_stats(stat_a, a_send, a_recv, True)
+    load_w.wait()
+
+    def first_product(t, code):
+        entry = code % 8
+        zj = entry % 4
+        same = entry < 4
+        j = 2 * zj + jnp.where(same, x, 1 - x)
+
+        @pl.when(t > 0)
+        def _():
+            remote(
+                gath.at[block(j)], gath.at[block(j)], ag_x.at[0], ag_recv.at[j], dp=d + 1 - 2 * x
+            ).wait_recv()
+
+            @pl.when(same)
+            def _():
+                forward(j, zj)
+
+        mine = j // 4 == m
+        r = j % 4
+
+        def tile(n, carry):
+            part = jnp.dot(
+                gath[block(j), :], w[:, columns(n, 256)], preferred_element_type=f32
+            )
+
+            @pl.when(mine)
+            def _():
+                kept[block(r), columns(n, 256)] = part
+
+            @pl.when(jnp.logical_not(mine))
+            def _():
+                y_out[block(r), columns(n, 256)] = part.astype(bf16)
+
+            return carry
+
+        lax.fori_loop(0, width // 256, tile, 0)
+
+        @pl.when(jnp.logical_not(mine))
+        def _():
+            y_copy(r).start()
+
+        return code // 8
+
+    lax.fori_loop(0, 8, first_product, by_place(z, ARRIVALS))
+
+    receive_stats(stat_a, a_send, a_recv)
+    send_stats(stat_a, a_send, a_recv, False)
+
+    def totals(stats, r):
+        at = pl.ds(pl.multiple_of(r * 8, 8), 8)
+        total = stats[0, at, :]
+        for e in range(1, 8):
+            total = total + stats[e, at, :]
+        return as_columns(total)
+
+    def moments_of(stats, r):
+        first_sum, square_sum = totals(stats, r)
+        center = first_sum / D
+        spread = square_sum / D - center * center
+        return center, lax.rsqrt(spread + 1e-05)
+
+    def section_sums(i, carry):
+        r = (i + 2 * m) % 4
+        y_copy(r).wait_recv()
+        at = pl.ds(pl.multiple_of(r * 8, 8), 8)
+
+        @pl.when(first_section)
+        def _():
+            v = kept[block(r), :] + y_in[block(r), :].astype(f32) + saved[block(r), :].astype(f32)
+            v = v.astype(bf16)
+            rows[block(r), :] = v
+            v = v.astype(f32)
+            stat_b[d, at, :] = as_rows(
+                jnp.sum(v, axis=1, keepdims=True), jnp.sum(v * v, axis=1, keepdims=True)
+            )
+
+        @pl.when(jnp.logical_not(first_section))
+        def _():
+            center, inverse = moments_of(stat_a, r)
+            scaled = (kept[block(r), :] + y_in[block(r), :].astype(f32)) * gain[...]
+            kept[block(r), :] = scaled
+            normed = (saved[block(r), :].astype(f32) - center) * inverse
+            stat_b[d, at, :] = as_rows(
+                jnp.sum(scaled, axis=1, keepdims=True),
+                jnp.sum(scaled * normed, axis=1, keepdims=True),
+            )
+
+        return carry
+
+    lax.fori_loop(0, 4, section_sums, 0)
+    send_stats(stat_b, b_send, b_recv, True)
+
+    def drain(zj, carry):
+        j = 2 * zj + x
+
+        @pl.when((zj <= z) & (z < 3))
+        def _():
+            upward(j, zj).wait_send()
+
+        @pl.when((zj >= z) & (z > 0))
+        def _():
+            downward(j, zj).wait_send()
+
+        over_x(j, zj).wait_send()
+        y_copy(zj).wait_send()
+        return carry
+
+    lax.fori_loop(0, 4, drain, 0)
+    receive_stats(stat_b, b_send, b_recv)
+    send_stats(stat_b, b_send, b_recv, False)
+
+    def operand_near(r):
+        b = 4 * m + r
+        return remote(
+            operand.at[block(r)], operands.at[block(b)], o_send.at[r], o_recv.at[b], section=1 - s
+        )
+
+    def operand_far(r):
+        b = 4 * m + r
+        return remote(
+            operand.at[block(r)], operands.at[block(b)], o_cross.at[r], o_recv.at[b],
+            section=1 - s, mp=1 - m,
+        )
+
+    def hand_over(r):
+        return remote(
+            rows.at[block(r)], handed.at[block(r)], h_send.at[r], h_recv.at[r], section=1 - s
+        )
+
+    def finish_rows(i, carry):
+        r = (i + 2 * m) % 4
+
+        @pl.when(first_section)
+        def _():
+            center, inverse = moments_of(stat_b, r)
+            v = rows[block(r), :].astype(f32)
+            operand[block(r), :] = ((v - center) * inverse * gain[...] + bias[...]).astype(bf16)
+
+        @pl.when(jnp.logical_not(first_section))
+        def _():
+            center, inverse = moments_of(stat_a, r)
+            first_total, second_total = totals(stat_b, r)
+            normed = (saved[block(r), :].astype(f32) - center) * inverse
+            v = inverse * (kept[block(r), :] - first_total / D - normed * (second_total / D))
+            v = v.astype(bf16)
+            rows[block(r), :] = v
+            operand[block(r), :] = v
+
+        operand_far(r).start()
+        operand_near(r).start()
+        return carry
+
+    lax.fori_loop(0, 4, finish_rows, 0)
+
+    def x_copy(zj):
+        return remote(
+            gath.at[block(2 * zj + 1 - x)], x_in.at[block(zj)], xs_send.at[zj], xs_recv.at[zj],
+            dp=d + 1 - 2 * x,
+        )
+
+    def second_product(i, code):
+        zj = code % 8
+        for k in range(2):
+            b = 2 * zj + k
+            remote(
+                operand.at[block(0)], operands.at[block(b)], o_send.at[0], o_recv.at[b],
+                section=1 - s,
+            ).wait_recv()
+
+        def tile(n, carry):
+            part = lax.dot_general(
+                operands[block(2 * zj, 2), :], w[columns(n, 256), :],
+                (((1,), (1,)), ((), ())), preferred_element_type=f32,
+            )
+            gath[block(2 * zj, 2), columns(n, 256)] = part.astype(bf16)
+            return carry
+
+        lax.fori_loop(0, depth // 256, tile, 0)
+        x_copy(zj).start()
+        return code // 8
+
+    lax.fori_loop(0, 4, second_product, by_place(z, DESTINATIONS))
+
+    def hand(r, carry):
+        hand_over(r).start()
+        return carry
+
+    lax.fori_loop(0, 4, hand, 0)
+
+    def z_up(zj):
+        return remote(
+            x_in.at[block(zj)], z_in.at[block(zj)], zs_send.at[zj], zs_recv.at[zj], dp=(d + 2) % 8
+        )
+
+    def z_down(zj):
+        slot = jnp.where(zj == z - 1, 4, zj)
+        return remote(
+            x_in.at[block(zj)], z_in.at[block(slot)], zs_send.at[zj], zs_recv.at[slot], dp=(d + 6) % 8
+        )
+
+    def arrived(slot):
+        remote(
+            x_in.at[block(0)], z_in.at[block(slot)], zs_send.at[0], zs_recv.at[slot], dp=(d + 2) % 8
+        ).wait_recv()
+
+    def gather_sums(i, code):
+        zj = code % 8
+        x_copy(zj).wait_recv()
+        own = zj == z
+        one = ((zj >= z) & (z > 0)) | ((zj < z) & (z < 3))
+        two = own & (z < 3)
+
+        @pl.when(one)
+        def _():
+            arrived(zj)
+
+        @pl.when(two)
+        def _():
+            arrived(4)
+
+        def add(with_one, with_two):
+            def tile(n, carry):
+                c = columns(n, 512)
+                total = gath[block(2 * zj + x), c].astype(f32) + x_in[block(zj), c].astype(f32)
+                if with_one:
+                    total = total + z_in[block(zj), c].astype(f32)
+                if with_two:
+                    total = total + z_in[block(4), c].astype(f32)
+                x_in[block(zj), c] = total.astype(bf16)
+                return carry
+
+            lax.fori_loop(0, depth // 512, tile, 0)
+
+        for with_one in (False, True):
+            for with_two in (False, True):
+                a = one if with_one else jnp.logical_not(one)
+                b = two if with_two else jnp.logical_not(two)
+                pl.when(a & b)(functools.partial(add, with_one, with_two))
+
+        @pl.when(zj > z)
+        def _():
+            z_up(zj).start()
+
+        @pl.when(zj < z)
+        def _():
+            z_down(zj).start()
+
+        return code // 8
+
+    lax.fori_loop(0, 4, gather_sums, by_place(z, DESTINATIONS))
+    store = pltpu.make_async_copy(x_in.at[block(z)], result, local_sem.at[2])
+    store.start()
+
+    def finish(r, carry):
+        hand_over(r).wait()
+        operand_near(r).wait_send()
+        operand_far(r).wait_send()
+        x_copy(r).wait_send()
+
+        @pl.when(r > z)
+        def _():
+            z_up(r).wait_send()
+
+        @pl.when(r < z)
+        def _():
+            z_down(r).wait_send()
+
+        return carry
+
+    lax.fori_loop(0, 4, finish, 0)
+    store.wait()
+
+
+def fused_local(section_weights, tensor_inputs, stream_inputs, ln_gain, ln_bias):
+    weight = section_weights[0]
+    incoming = tensor_inputs[0]
+    saved = stream_inputs[0]
+    depth, width = weight.shape
+    bf16, f32 = jnp.bfloat16, jnp.float32
+    sem = pltpu.SemaphoreType.DMA
+    anywhere = pl.BlockSpec(memory_space=pl.ANY)
+    vmem = pl.BlockSpec(memory_space=pltpu.VMEM)
+    handed, result = pl.pallas_call(
+        kernel,
+        out_shape=(
+            jax.ShapeDtypeStruct(saved.shape, bf16),
+            jax.ShapeDtypeStruct(incoming.shape, bf16),
+        ),
+        in_specs=[anywhere, anywhere, vmem, vmem, vmem],
+        out_specs=(anywhere, anywhere),
+        scratch_shapes=[
+            pltpu.VMEM((depth, width), bf16),
+            pltpu.VMEM((1024, depth), bf16),
+            pltpu.VMEM((512, width), f32),
+            pltpu.VMEM((512, width), bf16),
+            pltpu.VMEM((512, width), bf16),
+            pltpu.VMEM((512, width), bf16),
+            pltpu.VMEM((512, width), bf16),
+            pltpu.VMEM((1024, width), bf16),
+            pltpu.VMEM((512, depth), bf16),
+            pltpu.VMEM((640, depth), bf16),
+            pltpu.VMEM((8, 32, 128), f32),
+            pltpu.VMEM((8, 32, 128), f32),
+            sem((3,)), sem((8,)), sem((4,)), sem((4,)), sem((4,)), sem((4,)), sem((4,)),
+            sem((8,)), sem((8,)), sem((8,)), sem((8,)),
+            sem((4,)), sem((4,)), sem((4,)), sem((4,)), sem((8,)),
+            sem((4,)), sem((4,)), sem((4,)), sem((5,)),
+        ],
+        compiler_params=pltpu.CompilerParams(
+            collective_id=0, has_side_effects=True, vmem_limit_bytes=64 * 1024 * 1024 - 65536
+        ),
+        cost_estimate=pl.CostEstimate(
+            flops=4 * 1024 * depth * width, bytes_accessed=2 * depth * width, transcendentals=0
+        ),
+    )(weight, incoming, saved, ln_gain[None], ln_bias[None])
+    return handed[None], result[None]
+
+
 def solution(mesh):
+    fused = dict(mesh.shape) == {"section": 2, "dp": 8, "mp": 2}
     in_specs = (
         P("section", "mp", "dp"),
         P("section", "dp", "mp"),
@@ -71,4 +514,5 @@
         P("dp"),
     )
     out_specs = (P("section", "mp", "dp"), P("section", "dp", "mp"))
-    return jax.shard_map(local, mesh=mesh, in_specs=in_specs, out_specs=out_specs, check_vma=False)
+    body = fused_local if fused else local
+    return jax.shard_map(body, mesh=mesh, in_specs=in_specs, out_specs=out_specs, check_vma=False)

time: 826 us -> 337 us (0.41)
  waiting for transfers between devices: 699 us -> 0 us
  Pallas kernels: 0 us -> 326 us
  matrix products: 52.5 us -> 0 us
  blocking collectives: 38.5 us -> 0 us
  between operations: 13.8 us -> 0.65 us
  other arithmetic: 12.1 us -> 0 us
    reduce_scatter x2 -> x0, waiting for transfers between devices: 467 us -> none  [the longest x1 405 us: summed_output(): return lax.psum_scatter(product, 'dp', scatter_dimension=0, tiled=True)]
    pallas_call x0 -> x1, Pallas kernels: none -> 326 us  [fused_local(): pl.pallas_call(kernel, out_shape=(jax.ShapeDtypeStruct(saved.shape, bf16)...]
    all_gather x2 -> x0, waiting for transfers between devices: 229 us -> none  [the longest x1 178 us: local(): lax.all_gather(incoming, 'dp', axis=0, tiled=True)]
    dot_general x2 -> x0, matrix products: 52.5 us -> none  [the longest x1 26.3 us: contract(): lax.dot_general(left, weight, (((1,), (1,)), ((), ())), preferred_element...]
    psum x3 -> x0, blocking collectives: 38.5 us -> none  [the longest x2 26.2 us: moments(): lax.psum((jnp.sum(values, axis=1), jnp.sum(values * values, axis=1)), 'dp')]
  transfers between devices with their start and end apart: 5 -> 0, of which waited for: 5 -> 0; matrix products, arithmetic and copies ran while one was open for 0% -> 0% of each run, Pallas kernels for 0% -> 0%
where the time goes in v1:
time: 337 us; the launch traced here: 334 us
  Pallas kernels  326 us (97%)
  local copies, waits for them, and re-layouts  6.51 us (2%)
    pallas_call x1, Pallas kernels, fused_local(): pl.pallas_call(kernel, out_shape=(jax.ShapeDtypeStruct(saved.shape, bf16)...  326 us

profile of v1, /device:TPU:21, one launch (start us, length us, event | category | flops | bytes accessed | tf_op | source)
XLA Modules:
  0.0 333.6 jit_solution(7145706340702434685)
XLA Ops:
  0.6 1.3 broadcast_in_dim.12.gain
  1.9 1.3 broadcast_in_dim.13.bias
  3.2 326.5 %shard_map.68 = (bf16[512,1536]{1,0:T(8,128)(2,1)}, bf16[128,6144]{1,0:T(8,128)(2,1)}) custom-call(bf16[6144,1536]{1,0:T(8,128)(2,1)} %bitcast.7, bf16[128,6144]{1,0:T(8,128)(2,1)} %bitcast.8, bf16[512,1536]{1,0:T(8,128)(2,1)} %bitcast.9, f32[1,1536]{1,0:T(1,128)} %broadcast_in_dim.12.gain, f32[1,1536]{1,0:T(1,128)} %broadcast_in_dim.13.bias), custom_call_target="tpu_custom_call" | custom-call | flops 38654705664 | bytes 18874368 | tf_op jit(solution)/shard_map/pallas_call | solution.py:471
  329.7 0.0 copy-start
  329.7 2.8 copy.9
  332.5 0.0 copy-done
  332.5 1.1 copy.10
Async XLA Ops:
  329.7 2.8 copy-start

commit v2 on v1

--- a/solution.py
+++ b/solution.py
@@ -97,10 +97,11 @@
 def kernel(
     w_hbm, x_hbm, saved, gain, bias, handed, result,
     w, gath, kept, y_out, y_in, rows, operand, operands, x_in, z_in,
-    stat_a, stat_b,
+    zb_in, stat_a, stat_b,
     local_sem, ag_recv, ag_x, ag_up, ag_down, y_send, y_recv,
     a_send, a_recv, b_send, b_recv,
     h_send, h_recv, o_send, o_cross, o_recv, xs_send, xs_recv, zs_send, zs_recv,
+    ab_send, ab_recv, zb_send, zb_recv,
 ):
     s, d, m = lax.axis_index("section"), lax.axis_index("dp"), lax.axis_index("mp")
     z, x = d // 2, d % 2
@@ -111,6 +112,15 @@
 
     def block(j, n=1):
         return pl.ds(pl.multiple_of(j * 128, 128), 128 * n)
+
+    def half(j, h):
+        return pl.ds(pl.multiple_of(j * 128 + h * 64, 64), 64)
+
+    def is_edge(zj):
+        return (zj == 0) | (zj == 3)
+
+    def is_split(zj):
+        return is_edge(zj) & (zj != z)
 
     def columns(n, size):
         return pl.ds(pl.multiple_of(n * size, size), size)
@@ -137,8 +147,19 @@
     pl.semaphore_wait(barrier, 10)
     load_x.wait()
 
-    def over_x(j, zj):
-        return remote(gath.at[block(j)], gath.at[block(j)], ag_x.at[zj], ag_recv.at[j], dp=d + 1 - 2 * x)
+    def over_x(j, zj, at):
+        return remote(gath.at[at], gath.at[at], ag_x.at[zj], ag_recv.at[j], dp=d + 1 - 2 * x)
+
+    def whole_or_half(zj, j, act):
+        pl.when(is_split(zj))(lambda: act(half(j, 0)))
+        pl.when(jnp.logical_not(is_split(zj)))(lambda: act(block(j)))
+
+    def half_along_z(j, e, act):
+        def go(target):
+            act(remote(gath.at[half(j, 1)], gath.at[half(j, 1)], ab_send.at[e], ab_recv.at[e], dp=target))
+
+        pl.when((e == 0) & (z < 3))(lambda: go((d + 2) % 8))
+        pl.when((e == 1) & (z > 0))(lambda: go((d + 6) % 8))
 
     def upward(j, zj):
         return remote(gath.at[block(j)], gath.at[block(j)], ag_up.at[zj], ag_recv.at[j], dp=(d + 2) % 8)
@@ -171,7 +192,7 @@
         def _():
             downward(j, zj).start()
 
-        over_x(j, zj).start()
+        whole_or_half(zj, j, lambda at: over_x(j, zj, at).start())
 
     forward(d, z)
 
@@ -193,15 +214,31 @@
         same = entry < 4
         j = 2 * zj + jnp.where(same, x, 1 - x)
 
-        @pl.when(t > 0)
-        def _():
-            remote(
-                gath.at[block(j)], gath.at[block(j)], ag_x.at[0], ag_recv.at[j], dp=d + 1 - 2 * x
-            ).wait_recv()
+        other = jnp.logical_not(same)
+        parted = other & is_split(zj)
+        e = zj // 3
+
+        @pl.when((t > 0) & jnp.logical_not(parted))
+        def _():
+            over_x(j, zj, block(j)).wait_recv()
 
             @pl.when(same)
             def _():
                 forward(j, zj)
+
+        @pl.when(parted)
+        def _():
+            remote(
+                gath.at[half(j, 1)], gath.at[half(j, 1)], ab_send.at[e], ab_recv.at[e], dp=(d + 2) % 8
+            ).wait_recv()
+
+        @pl.when(other & is_edge(zj))
+        def _():
+            half_along_z(j, e, lambda c: c.start())
+
+        @pl.when(parted)
+        def _():
+            over_x(j, zj, half(j, 0)).wait_recv()
 
         mine = j // 4 == m
         r = j % 4
@@ -289,7 +326,12 @@
         def _():
             downward(j, zj).wait_send()
 
-        over_x(j, zj).wait_send()
+        whole_or_half(zj, j, lambda at: over_x(j, zj, at).wait_send())
+
+        @pl.when(is_edge(zj))
+        def _():
+            half_along_z(2 * zj + 1 - x, zj // 3, lambda c: c.wait_send())
+
         y_copy(zj).wait_send()
         return carry
 
@@ -340,11 +382,44 @@
 
     lax.fori_loop(0, 4, finish_rows, 0)
 
-    def x_copy(zj):
-        return remote(
-            gath.at[block(2 * zj + 1 - x)], x_in.at[block(zj)], xs_send.at[zj], xs_recv.at[zj],
-            dp=d + 1 - 2 * x,
-        )
+    def x_copy(zj, act):
+        def go(source, target):
+            act(
+                remote(
+                    gath.at[source], x_in.at[target], xs_send.at[zj], xs_recv.at[zj],
+                    dp=d + 1 - 2 * x,
+                )
+            )
+
+        j = 2 * zj + 1 - x
+        pl.when(is_split(zj))(lambda: go(half(j, 0), half(zj, 0)))
+        pl.when(jnp.logical_not(is_split(zj)))(lambda: go(block(j), block(zj)))
+
+    def half_sums(e, act):
+        def go(target):
+            act(
+                remote(
+                    gath.at[half(6 * e + 1 - x, 1)], zb_in.at[half(0, e)], zb_send.at[e],
+                    zb_recv.at[e], dp=target,
+                )
+            )
+
+        pl.when((e == 1) & (z < 3))(lambda: go((d + 2) % 8))
+        pl.when((e == 0) & (z > 0))(lambda: go((d + 6) % 8))
+
+    def add_half(e):
+        j = 6 * e + 1 - x
+        remote(
+            gath.at[half(j, 1)], zb_in.at[half(0, e)], zb_send.at[e], zb_recv.at[e], dp=(d + 2) % 8
+        ).wait_recv()
+
+        def tile(n, carry):
+            c = columns(n, 512)
+            total = gath[half(j, 1), c].astype(f32) + zb_in[half(0, e), c].astype(f32)
+            gath[half(j, 1), c] = total.astype(bf16)
+            return carry
+
+        lax.fori_loop(0, depth // 512, tile, 0)
 
     def second_product(i, code):
         zj = code % 8
@@ -364,10 +439,27 @@
             return carry
 
         lax.fori_loop(0, depth // 256, tile, 0)
-        x_copy(zj).start()
+        @pl.when(is_split(zj) & is_edge(z))
+        def _():
+            half_sums(zj // 3, lambda c: c.start())
+
+        @pl.when(jnp.logical_not(is_edge(zj) & (zj == z)))
+        def _():
+            x_copy(zj, lambda c: c.start())
+
         return code // 8
 
     lax.fori_loop(0, 4, second_product, by_place(z, DESTINATIONS))
+
+    @pl.when(jnp.logical_not(is_edge(z)))
+    def _():
+        def pass_on(i, carry):
+            e = (i + z) % 2
+            add_half(e)
+            half_sums(e, lambda c: c.start())
+            return carry
+
+        lax.fori_loop(0, 2, pass_on, 0)
 
     def hand(r, carry):
         hand_over(r).start()
@@ -393,7 +485,13 @@
 
     def gather_sums(i, code):
         zj = code % 8
-        x_copy(zj).wait_recv()
+
+        @pl.when((i == 2) & is_edge(z))
+        def _():
+            add_half(z // 3)
+            x_copy(z, lambda c: c.start())
+
+        x_copy(zj, lambda c: c.wait_recv())
         own = zj == z
         one = ((zj >= z) & (z > 0)) | ((zj < z) & (z < 3))
         two = own & (z < 3)
@@ -406,15 +504,17 @@
         def _():
             arrived(4)
 
-        def add(with_one, with_two):
+        def add(h, with_x, with_one, with_two):
             def tile(n, carry):
                 c = columns(n, 512)
-                total = gath[block(2 * zj + x), c].astype(f32) + x_in[block(zj), c].astype(f32)
+                total = gath[half(2 * zj + x, h), c].astype(f32)
+                if with_x:
+                    total = total + x_in[half(zj, h), c].astype(f32)
                 if with_one:
-                    total = total + z_in[block(zj), c].astype(f32)
+                    total = total + z_in[half(zj, h), c].astype(f32)
                 if with_two:
-                    total = total + z_in[block(4), c].astype(f32)
-                x_in[block(zj), c] = total.astype(bf16)
+                    total = total + z_in[half(4, h), c].astype(f32)
+                x_in[half(zj, h), c] = total.astype(bf16)
                 return carry
 
             lax.fori_loop(0, depth // 512, tile, 0)
@@ -423,7 +523,11 @@
             for with_two in (False, True):
                 a = one if with_one else jnp.logical_not(one)
                 b = two if with_two else jnp.logical_not(two)
-                pl.when(a & b)(functools.partial(add, with_one, with_two))
+                pl.when(a & b)(functools.partial(add, 0, True, with_one, with_two))
+                for with_x in (False, True):
+                    if with_x or not with_two:
+                        c = jnp.logical_not(is_split(zj)) if with_x else is_split(zj)
+                        pl.when(a & b & c)(functools.partial(add, 1, with_x, with_one, with_two))
 
         @pl.when(zj > z)
         def _():
@@ -443,7 +547,11 @@
         hand_over(r).wait()
         operand_near(r).wait_send()
         operand_far(r).wait_send()
-        x_copy(r).wait_send()
+        x_copy(r, lambda c: c.wait_send())
+
+        @pl.when(r < 2)
+        def _():
+            half_sums(r, lambda c: c.wait_send())
 
         @pl.when(r > z)
         def _():
@@ -487,12 +595,14 @@
             pltpu.VMEM((1024, width), bf16),
             pltpu.VMEM((512, depth), bf16),
             pltpu.VMEM((640, depth), bf16),
+            pltpu.VMEM((128, depth), bf16),
             pltpu.VMEM((8, 32, 128), f32),
             pltpu.VMEM((8, 32, 128), f32),
             sem((3,)), sem((8,)), sem((4,)), sem((4,)), sem((4,)), sem((4,)), sem((4,)),
             sem((8,)), sem((8,)), sem((8,)), sem((8,)),
             sem((4,)), sem((4,)), sem((4,)), sem((4,)), sem((8,)),
             sem((4,)), sem((4,)), sem((4,)), sem((5,)),
+            sem((2,)), sem((2,)), sem((2,)), sem((2,)),
         ],
         compiler_params=pltpu.CompilerParams(
             collective_id=0, has_side_effects=True, vmem_limit_bytes=64 * 1024 * 1024 - 65536

time: 337 us -> 319 us (0.947)
  Pallas kernels: 326 us -> 311 us
    pallas_call x1, Pallas kernels: 326 us -> 311 us  [fused_local(): pl.pallas_call(kernel, out_shape=(jax.ShapeDtypeStruct(saved.shape, bf16)...]
where the time goes in v2:
time: 319 us
  Pallas kernels  311 us (97%)
  local copies, waits for them, and re-layouts  6.51 us (2%)
    pallas_call x1, Pallas kernels, fused_local(): pl.pallas_call(kernel, out_shape=(jax.ShapeDtypeStruct(saved.shape, bf16)...  311 us

profile of v2, /device:TPU:21, one launch (start us, length us, event | category | flops | bytes accessed | tf_op | source)
XLA Modules:
  0.0 318.5 jit_solution(12757913310819779959)
XLA Ops:
  0.6 1.3 broadcast_in_dim.12.gain
  1.9 1.3 broadcast_in_dim.13.bias
  3.2 311.4 %shard_map.68 = (bf16[512,1536]{1,0:T(8,128)(2,1)}, bf16[128,6144]{1,0:T(8,128)(2,1)}) custom-call(bf16[6144,1536]{1,0:T(8,128)(2,1)} %bitcast.7, bf16[128,6144]{1,0:T(8,128)(2,1)} %bitcast.8, bf16[512,1536]{1,0:T(8,128)(2,1)} %bitcast.9, f32[1,1536]{1,0:T(1,128)} %broadcast_in_dim.12.gain, f32[1,1536]{1,0:T(1,128)} %broadcast_in_dim.13.bias), custom_call_target="tpu_custom_call" | custom-call | flops 38654705664 | bytes 18874368 | tf_op jit(solution)/shard_map/pallas_call | solution.py:579
  314.6 0.0 copy-start
  314.6 2.8 copy.9
  317.4 0.0 copy-done
  317.4 1.1 copy.10
Async XLA Ops:
  314.6 2.8 copy-start

commit v3 on v2

--- a/solution.py
+++ b/solution.py
@@ -358,7 +358,7 @@
         )
 
     def finish_rows(i, carry):
-        r = (i + 2 * m) % 4
+        r = 2 * ((i // 2 + m) % 2) + 1 - x + (i % 2) * (2 * x - 1)
 
         @pl.when(first_section)
         def _():
@@ -421,24 +421,34 @@
 
         lax.fori_loop(0, depth // 512, tile, 0)
 
+    def multiply(b, n_blocks):
+        for k in range(n_blocks):
+            remote(
+                operand.at[block(0)], operands.at[block(b + k)], o_send.at[0], o_recv.at[b + k],
+                section=1 - s,
+            ).wait_recv()
+
+        def tile(n, carry):
+            part = lax.dot_general(
+                operands[block(b, n_blocks), :], w[columns(n, 256), :],
+                (((1,), (1,)), ((), ())), preferred_element_type=f32,
+            )
+            gath[block(b, n_blocks), columns(n, 256)] = part.astype(bf16)
+            return carry
+
+        lax.fori_loop(0, depth // 256, tile, 0)
+
     def second_product(i, code):
         zj = code % 8
-        for k in range(2):
-            b = 2 * zj + k
-            remote(
-                operand.at[block(0)], operands.at[block(b)], o_send.at[0], o_recv.at[b],
-                section=1 - s,
-            ).wait_recv()
-
-        def tile(n, carry):
-            part = lax.dot_general(
-                operands[block(2 * zj, 2), :], w[columns(n, 256), :],
-                (((1,), (1,)), ((), ())), preferred_element_type=f32,
-            )
-            gath[block(2 * zj, 2), columns(n, 256)] = part.astype(bf16)
-            return carry
-
-        lax.fori_loop(0, depth // 256, tile, 0)
+
+        @pl.when(i == 0)
+        def _():
+            multiply(2 * zj + 1 - x, 1)
+
+        @pl.when(i > 0)
+        def _():
+            multiply(2 * zj, 2)
+
         @pl.when(is_split(zj) & is_edge(z))
         def _():
             half_sums(zj // 3, lambda c: c.start())
@@ -447,19 +457,9 @@
         def _():
             x_copy(zj, lambda c: c.start())
 
-        return code // 8
-
-    lax.fori_loop(0, 4, second_product, by_place(z, DESTINATIONS))
-
-    @pl.when(jnp.logical_not(is_edge(z)))
-    def _():
-        def pass_on(i, carry):
-            e = (i + z) % 2
-            add_half(e)
-            half_sums(e, lambda c: c.start())
-            return carry
-
-        lax.fori_loop(0, 2, pass_on, 0)
+        @pl.when(i == 0)
+        def _():
+            multiply(2 * zj + x, 1)
 
     def hand(r, carry):
         hand_over(r).start()
@@ -467,20 +467,29 @@
 
     lax.fori_loop(0, 4, hand, 0)
 
-    def z_up(zj):
+    def pass_on(i, carry):
+        e = (i + z) % 2
+        add_half(e)
+        half_sums(e, lambda c: c.start())
+        return carry
+
+    def z_up(zj, h):
         return remote(
-            x_in.at[block(zj)], z_in.at[block(zj)], zs_send.at[zj], zs_recv.at[zj], dp=(d + 2) % 8
+            x_in.at[half(zj, h)], z_in.at[half(zj, h)], zs_send.at[2 * zj + h],
+            zs_recv.at[2 * zj + h], dp=(d + 2) % 8,
         )
 
-    def z_down(zj):
+    def z_down(zj, h):
         slot = jnp.where(zj == z - 1, 4, zj)
         return remote(
-            x_in.at[block(zj)], z_in.at[block(slot)], zs_send.at[zj], zs_recv.at[slot], dp=(d + 6) % 8
+            x_in.at[half(zj, h)], z_in.at[half(slot, h)], zs_send.at[2 * zj + h],
+            zs_recv.at[2 * slot + h], dp=(d + 6) % 8,
         )
 
-    def arrived(slot):
+    def arrived(slot, h):
         remote(
-            x_in.at[block(0)], z_in.at[block(slot)], zs_send.at[0], zs_recv.at[slot], dp=(d + 2) % 8
+            x_in.at[half(0, h)], z_in.at[half(slot, h)], zs_send.at[h], zs_recv.at[2 * slot + h],
+            dp=(d + 2) % 8,
         ).wait_recv()
 
     def gather_sums(i, code):
@@ -495,14 +504,6 @@
         own = zj == z
         one = ((zj >= z) & (z > 0)) | ((zj < z) & (z < 3))
         two = own & (z < 3)
-
-        @pl.when(one)
-        def _():
-            arrived(zj)
-
-        @pl.when(two)
-        def _():
-            arrived(4)
 
         def add(h, with_x, with_one, with_two):
             def tile(n, carry):
@@ -519,27 +520,44 @@
 
             lax.fori_loop(0, depth // 512, tile, 0)
 
-        for with_one in (False, True):
-            for with_two in (False, True):
-                a = one if with_one else jnp.logical_not(one)
-                b = two if with_two else jnp.logical_not(two)
-                pl.when(a & b)(functools.partial(add, 0, True, with_one, with_two))
-                for with_x in (False, True):
-                    if with_x or not with_two:
-                        c = jnp.logical_not(is_split(zj)) if with_x else is_split(zj)
-                        pl.when(a & b & c)(functools.partial(add, 1, with_x, with_one, with_two))
-
-        @pl.when(zj > z)
-        def _():
-            z_up(zj).start()
-
-        @pl.when(zj < z)
-        def _():
-            z_down(zj).start()
-
-        return code // 8
-
-    lax.fori_loop(0, 4, gather_sums, by_place(z, DESTINATIONS))
+        for h in (0, 1):
+            pl.when(one)(lambda: arrived(zj, h))
+            pl.when(two)(lambda: arrived(4, h))
+            for with_one in (False, True):
+                for with_two in (False, True):
+                    a = one if with_one else jnp.logical_not(one)
+                    b = two if with_two else jnp.logical_not(two)
+                    if h == 0:
+                        pl.when(a & b)(functools.partial(add, 0, True, with_one, with_two))
+                        continue
+                    for with_x in (False, True):
+                        if with_x or not with_two:
+                            c = jnp.logical_not(is_split(zj)) if with_x else is_split(zj)
+                            pl.when(a & b & c)(
+                                functools.partial(add, 1, with_x, with_one, with_two)
+                            )
+            pl.when(zj > z)(lambda: z_up(zj, h).start())
+            pl.when(zj < z)(lambda: z_down(zj, h).start())
+
+    def sums_step(i, codes):
+        product_code, sum_code = codes
+
+        @pl.when(i < 4)
+        def _():
+            second_product(i, product_code)
+
+        @pl.when((i == 2) & jnp.logical_not(is_edge(z)))
+        def _():
+            lax.fori_loop(0, 2, pass_on, 0)
+
+        @pl.when(i >= 2)
+        def _():
+            gather_sums(i - 2, sum_code)
+
+        return product_code // 8, jnp.where(i >= 2, sum_code // 8, sum_code)
+
+    order = by_place(z, DESTINATIONS)
+    lax.fori_loop(0, 6, sums_step, (order, order))
     store = pltpu.make_async_copy(x_in.at[block(z)], result, local_sem.at[2])
     store.start()
 
@@ -555,11 +573,13 @@
 
         @pl.when(r > z)
         def _():
-            z_up(r).wait_send()
+            for h in (0, 1):
+                z_up(r, h).wait_send()
 
         @pl.when(r < z)
         def _():
-            z_down(r).wait_send()
+            for h in (0, 1):
+                z_down(r, h).wait_send()
 
         return carry
 
@@ -601,7 +621,7 @@
             sem((3,)), sem((8,)), sem((4,)), sem((4,)), sem((4,)), sem((4,)), sem((4,)),
             sem((8,)), sem((8,)), sem((8,)), sem((8,)),
             sem((4,)), sem((4,)), sem((4,)), sem((4,)), sem((8,)),
-            sem((4,)), sem((4,)), sem((4,)), sem((5,)),
+            sem((4,)), sem((4,)), sem((8,)), sem((10,)),
             sem((2,)), sem((2,)), sem((2,)), sem((2,)),
         ],
         compiler_params=pltpu.CompilerParams(

time: 319 us -> 308 us (0.966)
  Pallas kernels: 311 us -> 301 us
    pallas_call x1, Pallas kernels: 311 us -> 301 us  [fused_local(): pl.pallas_call(kernel, out_shape=(jax.ShapeDtypeStruct(saved.shape, bf16)...]
where the time goes in v3:
time: 308 us
  Pallas kernels  301 us (98%)
  local copies, waits for them, and re-layouts  6.51 us (2%)
    pallas_call x1, Pallas kernels, fused_local(): pl.pallas_call(kernel, out_shape=(jax.ShapeDtypeStruct(saved.shape, bf16)...  301 us

profile of v3, /device:TPU:21, one launch (start us, length us, event | category | flops | bytes accessed | tf_op | source)
XLA Modules:
  0.0 308.2 jit_solution(16728419684565030928)
XLA Ops:
  0.6 1.3 broadcast_in_dim.12.gain
  1.9 1.3 broadcast_in_dim.13.bias
  3.2 301.1 %shard_map.68 = (bf16[512,1536]{1,0:T(8,128)(2,1)}, bf16[128,6144]{1,0:T(8,128)(2,1)}) custom-call(bf16[6144,1536]{1,0:T(8,128)(2,1)} %bitcast.7, bf16[128,6144]{1,0:T(8,128)(2,1)} %bitcast.8, bf16[512,1536]{1,0:T(8,128)(2,1)} %bitcast.9, f32[1,1536]{1,0:T(1,128)} %broadcast_in_dim.12.gain, f32[1,1536]{1,0:T(1,128)} %broadcast_in_dim.13.bias), custom_call_target="tpu_custom_call" | custom-call | flops 38654705664 | bytes 18874368 | tf_op jit(solution)/shard_map/pallas_call | solution.py:599
  304.3 0.0 copy-start
  304.3 2.8 copy.9
  307.1 0.0 copy-done
  307.1 1.1 copy.10
Async XLA Ops:
  304.3 2.8 copy-start
